TPU v7x, 32 devices: a whole 2x2x4 slice. The times are simulated.
32 devices in a mesh: parts: 2 (over x), row: 8 (over z, y), col: 2 (over core).
Axes of the slice: x: 2, y: 2, z: 4, core: 2. Of those that a mesh axis runs over, the one named last changes fastest.
Arguments:
- tokens: bfloat16 [64, 512, 512], P(('parts', 'row'), 'col'), parts along dimension 0, may hold values from -6 to 6
- expand_weight: bfloat16 [512, 2048], replicated, may hold values from -0.25 to 0.25
- depth_kernel: float32 [3, 3, 2048], replicated, may hold values from -2 to 2
- project_weight: bfloat16 [2048, 512], replicated, may hold values from -0.125 to 0.125
- norm_gain: float32 [512], replicated, may hold values from 0.25 to 1.75
- attend_weight: bfloat16 [512, 1536], replicated, may hold values from -3 to 3
- output_weight: bfloat16 [512, 512], replicated, may hold values from -0.25 to 0.25
Outputs:
- section_out: bfloat16 [64, 512, 512], P(('parts', 'row'), 'col'), parts along dimension 0
There are 2 independent parts, one for each index of `parts`. A program takes and returns all parts, laid end to end along the dimension named above; an argument that names none is the same for every part. Nothing has to cross between parts.
All inputs are finite; a program needn't handle non-finite values.
Results may differ from a plain program's by a relative error of at most 0.012.
Values may be sent and summed in bfloat16 or wider, within the bound.
A program may use at most 128 MiB of HBM per device.

v0:
```python
import math

import jax
import jax.numpy as jnp
from jax import lax
from jax.sharding import PartitionSpec as P

HEADS = 16
HEAD_DIM = 32
GRID = 16


def extended(cells, sides, width):
    for axis, dim in sides:
        count = lax.axis_size(axis)
        ends = count - 1
        head = lax.slice_in_dim(cells, 0, width, axis=dim)
        tail = lax.slice_in_dim(cells, cells.shape[dim] - width, cells.shape[dim], axis=dim)
        cells = jnp.concatenate(
            [
                lax.ppermute(tail, axis, [(i, (i + 1) % count) for i in range(ends)]),
                cells,
                lax.ppermute(head, axis, [((i + 1) % count, i) for i in range(ends)]),
            ],
            axis=dim,
        )
    return cells


def gelu_tanh(values):
    return jax.nn.gelu(values, approximate=True)


def expand_tile(inputs, expand_weight):
    shape = inputs.shape
    product = jnp.dot(
        inputs.reshape(-1, shape[2]), expand_weight, preferred_element_type=jnp.float32
    )
    return gelu_tanh(product).astype(jnp.bfloat16).reshape(shape[0], shape[1], -1)


def layer_norm(values, gain):
    values = values.astype(jnp.float32)
    center = jnp.mean(values, axis=-1, keepdims=True)
    spread = jnp.mean((values - center) ** 2, axis=-1, keepdims=True)
    return ((values - center) * lax.rsqrt(spread + 1e-05) * gain).astype(jnp.bfloat16)


def attend_groups(groups, attend_weight, output_weight):
    count, members, channels = groups.shape
    projected = jnp.dot(
        groups.reshape(count * members, channels), attend_weight, preferred_element_type=jnp.float32
    )
    projected = projected.astype(jnp.bfloat16).reshape(count, members, 3, HEADS, HEAD_DIM)
    query_heads = projected[:, :, 0]
    key_heads = projected[:, :, 1]
    value_heads = projected[:, :, 2]
    scores = jnp.einsum(
        "nqhd,nkhd->nhqk", query_heads, key_heads, preferred_element_type=jnp.float32
    ) / math.sqrt(HEAD_DIM)
    soft = jax.nn.softmax(scores, axis=-1).astype(jnp.bfloat16)
    heads_out = jnp.einsum("nhqk,nkhd->nqhd", soft, value_heads, preferred_element_type=jnp.float32)
    heads_out = heads_out.astype(jnp.bfloat16).reshape(count * members, channels)
    result = jnp.dot(heads_out, output_weight, preferred_element_type=jnp.float32).astype(
        jnp.bfloat16
    )
    return result.reshape(count, members, channels)


def local(
    tokens, expand_weight, depth_kernel, project_weight, norm_gain, attend_weight, output_weight
):
    tile_rows, tile_cols, channels = tokens.shape
    padded_in = extended(tokens, (("row", 0), ("col", 1)), 1)
    expanded = expand_tile(padded_in, expand_weight)
    total = jnp.zeros((tile_rows, tile_cols, expanded.shape[2]), jnp.float32)
    for shift_row in range(3):
        for shift_col in range(3):
            total = (
                total
                + expanded[
                    shift_row : shift_row + tile_rows, shift_col : shift_col + tile_cols
                ].astype(jnp.float32)
                * depth_kernel[shift_row, shift_col]
            )
    depth = gelu_tanh(total).astype(jnp.bfloat16)
    branch = jnp.dot(
        depth.reshape(tile_rows * tile_cols, -1), project_weight, preferred_element_type=jnp.float32
    )
    mbconv = (tokens.astype(jnp.float32) + branch.reshape(tile_rows, tile_cols, channels)).astype(
        jnp.bfloat16
    )
    normed = layer_norm(mbconv, norm_gain)
    row_count = lax.axis_size("row")
    col_count = lax.axis_size("col")
    devices = row_count * col_count
    stride_rows = tile_rows * row_count // GRID
    stride_cols = tile_cols * col_count // GRID
    col_blocks = tile_cols // stride_cols
    if row_count % GRID == 0:
        spread_count = stride_rows // tile_rows
        per_dest = tile_rows * stride_cols // devices
        ordered = normed.reshape(tile_rows, col_blocks, stride_cols, channels).transpose(0, 2, 1, 3)
        ordered = ordered.reshape(devices, per_dest, col_blocks, channels)
    else:
        spread_count = 1
        row_blocks = tile_rows // stride_rows
        ordered = normed.reshape(
            row_blocks, stride_rows, col_blocks, stride_cols, channels
        ).transpose(1, 3, 0, 2, 4)
        ordered = ordered.reshape(devices, -1, row_blocks * col_blocks, channels)
    piece = lax.all_to_all(ordered, ("row", "col"), split_axis=0, concat_axis=0, tiled=True)
    items = piece.shape[1]
    per_source = piece.shape[2]
    grouped = piece.reshape(
        row_count // spread_count, spread_count, col_count, items, per_source, channels
    )
    grouped = grouped.transpose(3, 1, 0, 2, 4, 5).reshape(items * spread_count, -1, channels)
    result = attend_groups(grouped, attend_weight, output_weight)
    result = result.reshape(
        items, spread_count, row_count // spread_count, col_count, per_source, channels
    )
    returned = lax.all_to_all(
        result.transpose(2, 1, 3, 0, 4, 5).reshape(devices, items, per_source, channels),
        ("row", "col"),
        split_axis=0,
        concat_axis=0,
        tiled=True,
    )
    if row_count % GRID == 0:
        attention = returned.reshape(tile_rows, stride_cols, col_blocks, channels).transpose(
            0, 2, 1, 3
        )
    else:
        row_blocks = tile_rows // stride_rows
        attention = returned.reshape(
            stride_rows, stride_cols, row_blocks, col_blocks, channels
        ).transpose(2, 0, 3, 1, 4)
    attention = attention.reshape(tile_rows, tile_cols, channels)
    return (mbconv.astype(jnp.float32) + attention.astype(jnp.float32)).astype(jnp.bfloat16)


def solution(mesh):
    placed = (P(("parts", "row"), "col", None), P(), P(), P(), P(), P(), P())
    return jax.shard_map(
        local,
        mesh=mesh,
        in_specs=placed,
        out_specs=P(("parts", "row"), "col", None),
        check_vma=False,
    )
```

profile of v0, /device:TPU:13, one launch (start us, length us, event | category | flops | bytes accessed | tf_op | source)
XLA Modules:
  0.0 167.9 jit_solution(11963751496534343237)
XLA Ops:
  0.0 0.0 copy-start
  0.0 1.2 fusion.47
  1.2 3.1 %collective-permute-start = (bf16[1,256,512]{2,1,0:T(8,128)(2,1)S(1)}, bf16[1,256,512]{2,1,0:T(8,128)(2,1)S(1)}, u32[]{:S(2)}, u32[]{:S(2)}) collective-permute-start(bf16[1,256,512]{2,1,0:T(8,128)(2,1)S(1)} %get-tuple-element.11), channel_id=1, source_target_pairs={{0,2},{2,4},{4,6},{6,8},{8,10},{10,12},{12,14},{1,3},{3,5},{5,7},{... | collective-permute-start | bytes 786440 | tf_op jit(solution)/shard_map/ppermute | solution.py:21
  4.4 2.1 %collective-permute-start.1 = (bf16[1,256,512]{2,1,0:T(8,128)(2,1)S(1)}, bf16[1,256,512]{2,1,0:T(8,128)(2,1)S(1)}, u32[]{:S(2)}, u32[]{:S(2)}) collective-permute-start(bf16[1,256,512]{2,1,0:T(8,128)(2,1)S(1)} %get-tuple-element.10), channel_id=1, source_target_pairs={{2,0},{4,2},{6,4},{8,6},{10,8},{12,10},{14,12},{3,1},{5,3},{7,5},{... | collective-permute-start | bytes 786440 | tf_op jit(solution)/shard_map/ppermute | solution.py:23
  6.5 9.4 %collective-permute-done = bf16[1,256,512]{2,1,0:T(8,128)(2,1)S(1)} collective-permute-done((bf16[1,256,512]{2,1,0:T(8,128)(2,1)S(1)}, bf16[1,256,512]{2,1,0:T(8,128)(2,1)S(1)}, u32[]{:S(2)}, u32[]{:S(2)}) %collective-permute-start) | collective-permute-done | bytes 262176 | tf_op jit(solution)/shard_map/ppermute | solution.py:21
  15.9 1.3 constant_dynamic-update-slice_fusion.1
  17.2 0.0 collective-permute-done.1
  17.3 1.3 collective-permute-start.2
  18.6 3.5 %collective-permute-start.3 = (bf16[6,1,512]{2,1,0:T(2,128)(2,1)S(1)}, bf16[6,1,512]{2,1,0:T(2,128)(2,1)S(1)}, u32[]{:S(2)}, u32[]{:S(2)}) collective-permute-start(bf16[6,1,512]{2,1,0:T(2,128)(2,1)S(1)} %get-tuple-element.9), channel_id=1, source_target_pairs={{1,0},{3,2},{5,4},{7,6},{9,8},{11,10},{13,12},{15,14},{17,16},{19,... | collective-permute-start | bytes 18440 | tf_op jit(solution)/shard_map/ppermute | solution.py:23
  22.1 1.1 fusion.48
  23.1 0.0 collective-permute-done.2
  23.1 0.0 collective-permute-done.3
  23.1 1.6 pad_maximum_fusion
  24.7 2.7 %reshape.49 = bf16[1548,512]{1,0:T(8,128)(2,1)} reshape(bf16[6,258,512]{2,1,0:T(8,128)(2,1)} %pad_maximum_fusion) | data formatting | bytes 3170304 | tf_op jit(solution)/shard_map/reshape | solution.py:37
  27.4 0.0 copy-done
  27.4 9.0 %fusion.11 = bf16[1548,2048]{1,0:T(8,128)(2,1)} fusion(bf16[1548,512]{1,0:T(8,128)(2,1)} %reshape.49, bf16[512,2048]{1,0:T(8,128)(2,1)S(1)} %copy-done), kind=kOutput, calls=%fused_computation.13 | convolution fusion | flops 3274924032 | bytes 10022912 | tf_op jit(solution)/shard_map/dot_general | solution.py:36
  36.3 8.8 %reshape.50 = bf16[6,258,2048]{2,1,0:T(8,128)(2,1)} reshape(bf16[1548,2048]{1,0:T(8,128)(2,1)} %fusion.11) | data formatting | bytes 12681216 | tf_op jit(solution)/shard_map/reshape | solution.py:39
  45.1 0.0 copy-done.4
  45.1 26.2 %convert_reduce_fusion = (f32[4,256]{1,0:T(4,128)S(1)}, bf16[4,256,512]{2,1,0:T(8,128)(2,1)S(1)}) fusion(bf16[2048,512]{1,0:T(8,128)(2,1)} %param.10, bf16[6,258,2048]{2,1,0:T(8,128)(2,1)} %reshape.50, f32[2048]{0:T(1024)S(1)} %bitcast.90, f32[2048]{0:T(1024)S(1)} %bitcast.91, f32[2048]{0:T(1024)S(1)} %bitcast.84, f32[2048]{0:T(1024)S(1)} %bitcast.85, ...), kind=kOutput, calls=%fused_computation.30 | convolution fusion | flops 2223504384 | bytes 42020864 | tf_op jit(solution)/shard_map/dot_general | solution.py:87
  71.4 0.0 copy-start.2
  71.4 0.0 copy-start.7
  71.4 0.5 fusion.28
  71.9 0.4 copy-done.2
  72.3 0.0 copy-done.6
  72.3 0.4 fusion.30
  72.8 0.6 copy.12
  73.3 29.9 %all_to_all.10 = bf16[16,4,16,512]{3,2,1,0:T(8,128)(2,1)S(1)} all-to-all(bf16[16,4,16,512]{3,2,1,0:T(8,128)(2,1)S(1)} %bitcast.76), channel_id=1, replica_groups=mesh['parts'=2,'row'=8,'col'=2] {'row','col'}, dimensions={0} | all-to-all | bytes 2097152 | tf_op jit(solution)/shard_map/all_to_all | solution.py:112
  103.2 0.1 copy.13
  103.3 0.0 copy-done.7
  103.3 1.8 %convolution_convert_fusion = bf16[1024,1536]{1,0:T(8,128)(2,1)S(1)} fusion(bf16[1024,512]{1,0:T(8,128)(2,1)S(1)} %bitcast.80, bf16[512,1536]{1,0:T(8,128)(2,1)S(1)} %copy-done.7), kind=kOutput, calls=%fused_computation.27 | convolution fusion | flops 1612185600 | bytes 5767168 | tf_op jit(solution)/shard_map/dot_general | solution.py:51
  105.1 2.9 %copy.14 = bf16[1024,1536]{0,1:T(8,128)(2,1)} copy(bf16[1024,1536]{1,0:T(8,128)(2,1)S(1)} %convolution_convert_fusion) | data formatting | bytes 6291456 | tf_op jit(solution)/shard_map/convert_element_type | solution.py:54
  108.0 4.8 %reshape.54 = bf16[4,256,3,16,32]{1,0,4,3,2:T(4,128)(2,1)S(1)} reshape(bf16[1024,1536]{0,1:T(8,128)(2,1)} %copy.14) | data formatting | bytes 6291456 | tf_op jit(solution)/shard_map/reshape | solution.py:54
  112.8 2.6 %fusion.45 = (bf16[4,256,1,16,32]{1,0,4,3,2:T(4,128)(2,1)}, bf16[4,256,1,16,32]{1,0,4,3,2:T(4,128)(2,1)}, bf16[4,256,1,16,32]{1,0,4,3,2:T(4,128)(2,1)}) fusion(bf16[4,256,3,16,32]{1,0,4,3,2:T(4,128)(2,1)S(1)} %reshape.54), kind=kLoop, calls=%fused_computation.58 | loop fusion | bytes 6291456 | tf_op jit(solution)/shard_map/slice | solution.py:57
  115.4 10.4 %fusion.49 = (f32[4,16,256]{2,1,0:T(8,128)S(1)}, f32[4,16,256,256]{2,3,1,0:T(8,128)}) fusion(bf16[4,256,1,16,32]{1,0,4,3,2:T(4,128)(2,1)} %get-tuple-element.6, bf16[4,256,1,16,32]{1,0,4,3,2:T(4,128)(2,1)} %get-tuple-element.7), kind=kOutput, calls=%fused_computation.62 | convolution fusion | flops 281018624 | bytes 18939904 | tf_op jit(solution)/shard_map/sub | solution.py:61
  125.8 0.0 copy-done.5
  125.8 7.3 %fusion.38 = bf16[4,256,16,32]{1,3,2,0:T(8,128)(2,1)S(1)} fusion(f32[4,16,256,256]{2,3,1,0:T(8,128)} %get-tuple-element.24, f32[4,16,256]{2,1,0:T(8,128)S(1)} %get-tuple-element.23, bf16[4,256,1,16,32]{1,0,4,3,2:T(4,128)(2,1)S(1)} %copy-done.5), kind=kOutput, calls=%fused_computation.43 | convolution fusion | flops 277348352 | bytes 18939904 | tf_op jit(solution)/shard_map/nhqk,nkhd->nqhd/dot_general | solution.py:62
  133.1 0.9 copy.19
  134.0 0.2 copy.26
  134.2 0.0 copy-done.8
  134.2 0.8 convolution_convert_fusion.1
  135.0 0.0 copy-start.3
  135.0 0.1 copy.20
  135.1 0.0 copy-start.1
  135.1 29.9 %all_to_all.11 = bf16[16,4,16,512]{3,2,1,0:T(8,128)(2,1)S(1)} all-to-all(bf16[16,4,16,512]{3,2,1,0:T(8,128)(2,1)S(1)} %bitcast.79), channel_id=1, replica_groups=mesh['parts'=2,'row'=8,'col'=2] {'row','col'}, dimensions={0} | all-to-all | bytes 2097152 | tf_op jit(solution)/shard_map/all_to_all | solution.py:123
  165.0 0.3 convert_bitcast_fusion
  165.3 1.2 copy.21
  166.5 0.0 copy-done.3
  166.5 1.3 fusion.31
  (10 shorter events, 0.1 us)
Async XLA Ops:
  0.0 27.4 %copy-start = (bf16[512,2048]{1,0:T(8,128)(2,1)S(1)}, bf16[512,2048]{1,0:T(8,128)(2,1)}, u32[]{:S(2)}) copy-start(bf16[512,2048]{1,0:T(8,128)(2,1)} %param.8) | copy-start | bytes 6291460
  1.2 14.7 %collective-permute-start = (bf16[1,256,512]{2,1,0:T(8,128)(2,1)S(1)}, bf16[1,256,512]{2,1,0:T(8,128)(2,1)S(1)}, u32[]{:S(2)}, u32[]{:S(2)}) collective-permute-start(bf16[1,256,512]{2,1,0:T(8,128)(2,1)S(1)} %get-tuple-element.11), channel_id=1, source_target_pairs={{0,2},{2,4},{4,6},{6,8},{8,10},{10,12},{12,14},{1,3},{3,5},{5,7},{... | collective-permute-start | bytes 786440 | tf_op jit(solution)/shard_map/ppermute | solution.py:21
  4.4 12.9 %collective-permute-start.1 = (bf16[1,256,512]{2,1,0:T(8,128)(2,1)S(1)}, bf16[1,256,512]{2,1,0:T(8,128)(2,1)S(1)}, u32[]{:S(2)}, u32[]{:S(2)}) collective-permute-start(bf16[1,256,512]{2,1,0:T(8,128)(2,1)S(1)} %get-tuple-element.10), channel_id=1, source_target_pairs={{2,0},{4,2},{6,4},{8,6},{10,8},{12,10},{14,12},{3,1},{5,3},{7,5},{... | collective-permute-start | bytes 786440 | tf_op jit(solution)/shard_map/ppermute | solution.py:23
  17.3 5.8 %collective-permute-start.2 = (bf16[6,1,512]{2,1,0:T(2,128)(2,1)S(1)}, bf16[6,1,512]{2,1,0:T(2,128)(2,1)S(1)}, u32[]{:S(2)}, u32[]{:S(2)}) collective-permute-start(bf16[6,1,512]{2,1,0:T(2,128)(2,1)S(1)} %get-tuple-element.8), channel_id=1, source_target_pairs={{0,1},{2,3},{4,5},{6,7},{8,9},{10,11},{12,13},{14,15},{16,17},{18,... | collective-permute-start | bytes 18440 | tf_op jit(solution)/shard_map/ppermute | solution.py:21
  18.6 4.5 %collective-permute-start.3 = (bf16[6,1,512]{2,1,0:T(2,128)(2,1)S(1)}, bf16[6,1,512]{2,1,0:T(2,128)(2,1)S(1)}, u32[]{:S(2)}, u32[]{:S(2)}) collective-permute-start(bf16[6,1,512]{2,1,0:T(2,128)(2,1)S(1)} %get-tuple-element.9), channel_id=1, source_target_pairs={{1,0},{3,2},{5,4},{7,6},{9,8},{11,10},{13,12},{15,14},{17,16},{19,... | collective-permute-start | bytes 18440 | tf_op jit(solution)/shard_map/ppermute | solution.py:23
  36.3 8.8 %copy-start.4 = (bf16[4,256,512]{2,1,0:T(8,128)(2,1)S(1)}, bf16[4,256,512]{2,1,0:T(8,128)(2,1)}, u32[]{:S(2)}) copy-start(bf16[4,256,512]{2,1,0:T(8,128)(2,1)} %param.7) | copy-start | bytes 3145732
  45.1 27.2 %copy-start.6 = (f32[512]{0:T(512)S(1)}, f32[512]{0:T(512)}, u32[]{:S(2)}) copy-start(f32[512]{0:T(512)} %param.11) | copy-start | bytes 6148
  71.4 1.0 copy-start.2
  71.4 31.9 %copy-start.7 = (bf16[512,1536]{1,0:T(8,128)(2,1)S(1)}, bf16[512,1536]{1,0:T(8,128)(2,1)}, u32[]{:S(2)}) copy-start(bf16[512,1536]{1,0:T(8,128)(2,1)} %param.12) | copy-start | bytes 4718596
  115.4 10.4 %copy-start.5 = (bf16[4,256,1,16,32]{1,0,4,3,2:T(4,128)(2,1)S(1)}, bf16[4,256,1,16,32]{1,0,4,3,2:T(4,128)(2,1)}, u32[]{:S(2)}) copy-start(bf16[4,256,1,16,32]{1,0,4,3,2:T(4,128)(2,1)} %get-tuple-element.5) | copy-start | bytes 3145732
  125.8 8.5 %copy-start.8 = (bf16[512,512]{1,0:T(8,128)(2,1)S(1)}, bf16[512,512]{1,0:T(8,128)(2,1)}, u32[]{:S(2)}) copy-start(bf16[512,512]{1,0:T(8,128)(2,1)} %param.13) | copy-start | bytes 1572868
  135.0 31.5 %copy-start.3 = (bf16[4,256,512]{2,1,0:T(8,128)(2,1)S(1)}, bf16[4,256,512]{2,1,0:T(8,128)(2,1)}, u32[]{:S(2)}) copy-start(bf16[4,256,512]{2,1,0:T(8,128)(2,1)} %copy-done.2) | copy-start | bytes 3145732
  135.1 32.8 %copy-start.1 = (bf16[512,2048]{1,0:T(8,128)(2,1)S(1)}, bf16[512,2048]{1,0:T(8,128)(2,1)}, u32[]{:S(2)}) copy-start(bf16[512,2048]{1,0:T(8,128)(2,1)} %param.8) | copy-start | bytes 6291460
where the time goes:
time: 170 us; the launch traced here: 168 us
  blocking collectives  59.8 us (35%)
  matrix products  55.4 us (33%)
  local copies, waits for them, and re-layouts  28.9 us (17%)
  starting transfers between devices  10 us (6%)
  waiting for transfers between devices  9.4 us (6%)
  other arithmetic  4.13 us (2%)
    all_to_all x1, blocking collectives, local(): lax.all_to_all(result.transpose(2, 1, 3, 0, 4, 5).reshape(devices, items,...  29.9 us
    all_to_all x1, blocking collectives, local(): lax.all_to_all(ordered, ('row', 'col'), split_axis=0, concat_axis=0, tile...  29.9 us
    dot_general x1, matrix products, local(): jnp.dot(depth.reshape(tile_rows * tile_cols, -1), project_weight, preferr...  26.2 us
    sub x1, matrix products, attend_groups(): soft = jax.nn.softmax(scores, axis=-1).astype(jnp.bfloat16)  10.4 us
    ppermute x2, waiting for transfers between devices, extended(): lax.ppermute(tail, axis, [(i, (i + 1) % count) for i in range(ends)])  9.39 us
    dot_general x1, matrix products, expand_tile(): jnp.dot(inputs.reshape(-1, shape[2]), expand_weight, preferred_element_ty...  8.95 us
    reshape x1, local copies, waits for them, and re-layouts, expand_tile(): gelu_tanh(product).astype(jnp.bfloat16).reshape(shape[0], shape[1], -1)  8.79 us
    dot_general x1, matrix products, attend_groups(): jnp.einsum('nhqk,nkhd->nqhd', soft, value_heads, preferred_element_type=j...  7.34 us
  transfers between devices with their start and end apart: 4, of which 1 were waited for; matrix products, arithmetic and copies ran while one was open for 1% of the time, Pallas kernels for 0%

commit v1 on v0

v1 whole, which is shorter than its diff:
```python
import functools
import math

import jax
import jax.numpy as jnp
from jax import lax
from jax.experimental import pallas as pl
from jax.experimental.pallas import tpu as pltpu
from jax.sharding import PartitionSpec as P

HEADS = 16
HEAD_DIM = 32
GRID = 16
LANES = 128
MESH = pl.DeviceIdType.MESH


def gelu_tanh(values):
    half = 0.5 * values
    inner = values * (0.7978845608028654 + 0.035677408136300125 * (values * values))
    return half + half * jnp.tanh(inner)


def kernel(
    row_count,
    col_count,
    spread,
    blocks,
    row_order,
    x_ref,
    dk_ref,
    gain_ref,
    ew_hbm,
    pw_hbm,
    aw_hbm,
    ow_hbm,
    out_ref,
    ew,
    pw,
    aw,
    ow,
    hrows,
    ledge,
    redge,
    xe,
    expanded,
    depth,
    branch,
    mb,
    sendbuf,
    recvbuf,
    qkv,
    heads,
    backbuf,
    retbuf,
    weight_sem,
    halo_send,
    halo_recv,
    fwd_send,
    fwd_recv,
    back_send,
    back_recv,
):
    tile_rows, tile_tokens, channels = x_ref.shape
    hidden = ew.shape[1]
    kinds, per_kind, team, piece, _ = sendbuf.shape
    residues = tile_tokens // blocks
    group_count = piece // blocks
    row = lax.axis_index("row")
    col = lax.axis_index("col")
    total = row_count * col_count
    me = row * col_count + col
    own = (row // spread) * col_count + col

    def member(index):
        return {"row": (index // col_count) * spread + row % spread, "col": index % col_count}

    weights = [
        pltpu.make_async_copy(src, dst, weight_sem.at[i])
        for i, (src, dst) in enumerate(((ew_hbm, ew), (pw_hbm, pw), (aw_hbm, aw), (ow_hbm, ow)))
    ]
    for copy in weights:
        copy.start()

    barrier = pltpu.get_barrier_semaphore()

    def greet(step, carry):
        other = lax.rem(me + step, total)
        pl.semaphore_signal(
            barrier,
            inc=1,
            device_id={"row": other // col_count, "col": lax.rem(other, col_count)},
            device_id_type=MESH,
        )
        return carry

    lax.fori_loop(1, total, greet, 0)
    pl.semaphore_wait(barrier, total - 1)

    last = tile_rows - 1
    edge = ledge.shape[1]
    tail = pl.ds(tile_tokens - edge, edge)
    front = pl.ds(0, edge)
    up, down, left, right = row > 0, row < row_count - 1, col > 0, col < col_count - 1
    halos = [
        (right, left, 0, 1, x_ref.at[:, tail], ledge.at[pl.ds(1, tile_rows)]),
        (left, right, 0, -1, x_ref.at[:, front], redge.at[pl.ds(1, tile_rows)]),
        (down, up, 1, 0, x_ref.at[last], hrows.at[0]),
        (up, down, -1, 0, x_ref.at[0], hrows.at[1]),
        (down & right, up & left, 1, 1, x_ref.at[last, tail], ledge.at[0]),
        (up & right, down & left, -1, 1, x_ref.at[0, tail], ledge.at[tile_rows + 1]),
        (down & left, up & right, 1, -1, x_ref.at[last, front], redge.at[0]),
        (up & left, down & right, -1, -1, x_ref.at[0, front], redge.at[tile_rows + 1]),
    ]

    def halo_copy(i):
        _, _, dr, dc, src, dst = halos[i]
        return pltpu.make_async_remote_copy(
            src_ref=src,
            dst_ref=dst,
            send_sem=halo_send.at[i],
            recv_sem=halo_recv.at[i],
            device_id={"row": row + dr, "col": col + dc},
            device_id_type=MESH,
        )

    for i, (sends, receives, _, _, _, dst) in enumerate(halos):

        @pl.when(sends)
        def _():
            halo_copy(i).start()

        @pl.when(jnp.logical_not(receives))
        def _():
            dst[...] = jnp.zeros(dst.shape, dst.dtype)

    def await_halo(indices):
        for i in indices:

            @pl.when(halos[i][1])
            def _():
                halo_copy(i).wait_recv()

    def stage(slot, source, ext):
        place = lax.broadcasted_iota(jnp.int32, (blocks, channels), 0)
        after = source[pl.ds(tile_tokens - edge, edge), :].astype(jnp.float32)[edge - blocks :]
        before = source[pl.ds(0, edge), :].astype(jnp.float32)[:blocks]
        low = ledge[ext].astype(jnp.float32)[edge - 1 : edge]
        high = redge[ext].astype(jnp.float32)[0:1]
        low = jnp.where(place == 0, low, pltpu.roll(after, 1, 0))
        high = jnp.where(place == blocks - 1, high, pltpu.roll(before, blocks - 1, 0))
        xe[slot, pl.ds(0, tile_tokens), :] = source[...]
        xe[slot, pl.ds(tile_tokens, 2 * blocks), :] = jnp.concatenate([low, high], axis=0).astype(
            jnp.bfloat16
        )

    def expand(rows):
        for slot, ext in enumerate(rows):
            if ext == 0:
                stage(slot, hrows.at[0], ext)
            elif ext == tile_rows + 1:
                stage(slot, hrows.at[1], ext)
            else:
                stage(slot, x_ref.at[ext - 1], ext)
        width = 256

        def columns(n, carry):
            lanes = pl.ds(pl.multiple_of(n * width, width), width)
            for slot, ext in enumerate(rows):
                product = jnp.dot(xe[slot], ew[:, lanes], preferred_element_type=jnp.float32)
                product = gelu_tanh(product).reshape(residues + 2, blocks, width)
                expanded[ext, pl.ds(1, residues), :, lanes] = product[:residues]
                expanded[ext, 0, :, lanes] = product[residues]
                expanded[ext, residues + 1, :, lanes] = product[residues + 1]
            return carry

        lax.fori_loop(0, hidden // width, columns, 0)

    def mbconv_row(i):
        part = 8

        def channel(n, carry):
            lanes = pl.ds(pl.multiple_of(n * LANES, LANES), LANES)
            taps = [[dk_ref[dr, pl.ds(dc, 1), lanes] for dc in range(3)] for dr in range(3)]
            for start in range(0, residues, part):
                acc = None
                for dr in range(3):
                    window = expanded[i + dr, pl.ds(start, part + 2), :, lanes]
                    for dc in range(3):
                        term = window[dc : dc + part] * taps[dr][dc]
                        acc = term if acc is None else acc + term
                value = gelu_tanh(acc).reshape(part * blocks, LANES).astype(jnp.bfloat16)
                depth[pl.ds(start * blocks, part * blocks), lanes] = value
            return carry

        lax.fori_loop(0, hidden // LANES, channel, 0)
        width = 256

        def project(n, carry):
            lanes = pl.ds(pl.multiple_of(n * width, width), width)
            branch[:, lanes] = jnp.dot(depth[...], pw[:, lanes], preferred_element_type=jnp.float32)
            return carry

        lax.fori_loop(0, channels // width, project, 0)
        kind, step = i % kinds, i // kinds
        chunk = tile_tokens // 8

        def norm(n, carry):
            rows = pl.ds(pl.multiple_of(n * chunk, chunk), chunk)
            value = (x_ref[i, rows, :].astype(jnp.float32) + branch[rows, :]).astype(jnp.bfloat16)
            mb[i, rows, :] = value
            value = value.astype(jnp.float32)
            center = jnp.mean(value, axis=-1, keepdims=True)
            value = value - center
            scale = lax.rsqrt(jnp.mean(value * value, axis=-1, keepdims=True) + 1e-05)
            normed = (value * scale * gain_ref[...]).astype(jnp.bfloat16)
            count = chunk // piece
            sendbuf[kind, step, pl.ds(n * count, count)] = normed.reshape(count, piece, channels)
            return carry

        lax.fori_loop(0, tile_tokens // chunk, norm, 0)

        def send(n, carry):
            other = lax.rem(own + n, team)
            forward_copy(kind, step, other, own).start()
            return carry

        lax.fori_loop(1, team, send, 0)
        recvbuf[kind, step, own] = sendbuf[kind, step, own]

    def forward_copy(kind, step, other, slot):
        return pltpu.make_async_remote_copy(
            src_ref=sendbuf.at[kind, step, other],
            dst_ref=recvbuf.at[kind, step, slot],
            send_sem=fwd_send.at[kind, step, other],
            recv_sem=fwd_recv.at[kind, step, slot],
            device_id=member(other),
            device_id_type=MESH,
        )

    def back_copy(kind, other, slot):
        return pltpu.make_async_remote_copy(
            src_ref=backbuf.at[kind, :, other],
            dst_ref=retbuf.at[kind, :, slot],
            send_sem=back_send.at[kind, other],
            recv_sem=back_recv.at[kind, slot],
            device_id=member(other),
            device_id_type=MESH,
        )

    def attend(kind):
        def arrive(n, carry):
            other = lax.rem(own + n, team)
            for step in range(per_kind):
                forward_copy(kind, step, other, other).wait_recv()
            return carry

        lax.fori_loop(1, team, arrive, 0)
        members = per_kind * team * blocks
        scale = math.log2(math.e) / math.sqrt(HEAD_DIM)
        width = 256

        def projection(n, carry):
            lanes = pl.ds(pl.multiple_of(n * width, width), width)
            group_tokens = recvbuf[kind].reshape(per_kind * team * piece, channels)
            value = jnp.dot(group_tokens, aw[:, lanes], preferred_element_type=jnp.float32)
            value = value * jnp.where(n * width < channels, scale, 1.0)
            value = value.reshape(per_kind * team, piece, width)
            for g in range(group_count):
                one = value[:, g * blocks : (g + 1) * blocks].reshape(members, width)
                qkv[g, :, lanes] = one.astype(jnp.bfloat16)
            return carry

        lax.fori_loop(0, 3 * channels // width, projection, 0)
        per_block = LANES // HEAD_DIM
        head_of = lax.broadcasted_iota(jnp.int32, (members, LANES), 1) // HEAD_DIM
        ones = jnp.ones((members, LANES), jnp.bfloat16)
        for g in range(group_count):

            def head_block(n, carry):
                base = n * LANES
                lanes = pl.ds(pl.multiple_of(base, LANES), LANES)
                queries = qkv[g, :, lanes]
                keys = qkv[g, :, pl.ds(pl.multiple_of(base + channels, LANES), LANES)]
                values = qkv[g, :, pl.ds(pl.multiple_of(base + 2 * channels, LANES), LANES)]
                values = jnp.concatenate([values, ones], axis=1)
                result = jnp.zeros((members, LANES), jnp.float32)
                for h in range(per_block):
                    mask = (head_of == h).astype(jnp.float32).astype(jnp.bfloat16)
                    scores = lax.dot_general(
                        queries * mask,
                        keys,
                        (((1,), (1,)), ((), ())),
                        preferred_element_type=jnp.float32,
                    )
                    top = jnp.max(scores, axis=-1, keepdims=True)
                    soft = jnp.exp2(scores - top).astype(jnp.bfloat16)
                    both = jnp.dot(soft, values, preferred_element_type=jnp.float32)
                    result = jnp.where(head_of == h, both[:, :LANES] / both[:, LANES:], result)
                heads[:, pl.ds(g * blocks, blocks), lanes] = result.reshape(
                    per_kind * team, blocks, LANES
                )
                return carry

            lax.fori_loop(0, channels // LANES, head_block, 0)

        merged = heads[...].reshape(per_kind * team * piece, channels).astype(jnp.bfloat16)
        result = jnp.dot(merged, ow[...], preferred_element_type=jnp.float32)
        backbuf[kind] = result.astype(jnp.bfloat16).reshape(per_kind, team, piece, channels)

        def send(n, carry):
            back_copy(kind, lax.rem(own + n, team), own).start()
            return carry

        lax.fori_loop(1, team, send, 0)
        for step in range(per_kind):
            retbuf[kind, step, own] = backbuf[kind, step, own]

    def finish(kind):
        def arrive(n, carry):
            other = lax.rem(own + n, team)
            back_copy(kind, other, other).wait_recv()
            return carry

        lax.fori_loop(1, team, arrive, 0)
        for step in range(per_kind):
            i = step * kinds + kind
            attention = retbuf[kind, step].reshape(tile_tokens, channels).astype(jnp.float32)
            out_ref[i] = (mb[i].astype(jnp.float32) + attention).astype(jnp.bfloat16)

    weights[0].wait()
    await_halo((0, 1))
    expand([1, 2, 3])
    weights[1].wait()
    mbconv_row(row_order[0])
    await_halo(range(2, len(halos)))
    expand([*range(4, tile_rows + 2), 0])
    for i in row_order[1:]:
        mbconv_row(i)
    weights[2].wait()
    weights[3].wait()
    kind_order = list(dict.fromkeys(i % kinds for i in row_order))
    for kind in kind_order:
        attend(kind)
    for kind in kind_order:
        finish(kind)

    for i, (sends, *_) in enumerate(halos):

        @pl.when(sends)
        def _():
            halo_copy(i).wait_send()

    def drain(n, carry):
        other = lax.rem(own + n, team)
        for kind in range(kinds):
            for step in range(per_kind):
                forward_copy(kind, step, other, own).wait_send()
            back_copy(kind, other, own).wait_send()
        return carry

    lax.fori_loop(1, team, drain, 0)


def local(
    tokens, expand_weight, depth_kernel, project_weight, norm_gain, attend_weight, output_weight
):
    tile_rows, tile_cols, channels = tokens.shape
    hidden = expand_weight.shape[1]
    row_count = lax.axis_size("row")
    col_count = lax.axis_size("col")
    stride_rows = tile_rows * row_count // GRID
    stride_cols = tile_cols * col_count // GRID
    blocks = tile_cols // stride_cols
    spread = max(1, stride_rows // tile_rows)
    kinds = min(stride_rows, tile_rows)
    per_kind = tile_rows // kinds
    team = row_count // spread * col_count
    piece = stride_cols // team * blocks
    row_order = [i for i in range(1, tile_rows) if i % kinds == 1 % kinds]
    row_order += [i for i in range(tile_rows - 1, -1, -1) if i not in row_order]
    ordered = tokens.reshape(tile_rows, blocks, stride_cols, channels).transpose(0, 2, 1, 3)
    ordered = ordered.reshape(tile_rows, tile_cols, channels)
    bf16, f32 = jnp.bfloat16, jnp.float32
    exchange = (kinds, per_kind, team, piece, channels)
    out = pl.pallas_call(
        functools.partial(kernel, row_count, col_count, spread, blocks, row_order),
        out_shape=jax.ShapeDtypeStruct((tile_rows, tile_cols, channels), bf16),
        in_specs=[pl.BlockSpec(memory_space=pltpu.VMEM)] * 3
        + [pl.BlockSpec(memory_space=pl.ANY)] * 4,
        out_specs=pl.BlockSpec(memory_space=pltpu.VMEM),
        scratch_shapes=[
            pltpu.VMEM(expand_weight.shape, bf16),
            pltpu.VMEM(project_weight.shape, bf16),
            pltpu.VMEM(attend_weight.shape, bf16),
            pltpu.VMEM(output_weight.shape, bf16),
            pltpu.VMEM((2, tile_cols, channels), bf16),
            pltpu.VMEM((tile_rows + 2, 16, channels), bf16),
            pltpu.VMEM((tile_rows + 2, 16, channels), bf16),
            pltpu.VMEM((3, tile_cols + 2 * blocks, channels), bf16),
            pltpu.VMEM((tile_rows + 2, stride_cols + 2, blocks, hidden), f32),
            pltpu.VMEM((tile_cols, hidden), bf16),
            pltpu.VMEM((tile_cols, channels), f32),
            pltpu.VMEM((tile_rows, tile_cols, channels), bf16),
            pltpu.VMEM(exchange, bf16),
            pltpu.VMEM(exchange, bf16),
            pltpu.VMEM((piece // blocks, per_kind * team * blocks, 3 * channels), bf16),
            pltpu.VMEM((per_kind * team, piece, channels), f32),
            pltpu.VMEM(exchange, bf16),
            pltpu.VMEM(exchange, bf16),
            pltpu.SemaphoreType.DMA((4,)),
            pltpu.SemaphoreType.DMA((8,)),
            pltpu.SemaphoreType.DMA((8,)),
            pltpu.SemaphoreType.DMA((kinds, per_kind, team)),
            pltpu.SemaphoreType.DMA((kinds, per_kind, team)),
            pltpu.SemaphoreType.DMA((kinds, team)),
            pltpu.SemaphoreType.DMA((kinds, team)),
        ],
        compiler_params=pltpu.CompilerParams(
            collective_id=0, has_side_effects=True, vmem_limit_bytes=52 * 1024 * 1024
        ),
    )(
        ordered,
        depth_kernel,
        norm_gain.reshape(1, channels),
        expand_weight,
        project_weight,
        attend_weight,
        output_weight,
    )
    out = out.reshape(tile_rows, stride_cols, blocks, channels).transpose(0, 2, 1, 3)
    return out.reshape(tile_rows, tile_cols, channels)


def solution(mesh):
    placed = (P(("parts", "row"), "col", None), P(), P(), P(), P(), P(), P())
    return jax.shard_map(
        local,
        mesh=mesh,
        in_specs=placed,
        out_specs=P(("parts", "row"), "col", None),
        check_vma=False,
    )
```

time: 170 us -> 76.2 us (0.45); the launches traced: 168 us -> 76 us
  Pallas kernels: 0 us -> 71.8 us
  blocking collectives: 59.8 us -> 0 us
  matrix products: 55.4 us -> 0 us
  local copies, waits for them, and re-layouts: 28.9 us -> 4.15 us
  starting transfers between devices: 10 us -> 0 us
  waiting for transfers between devices: 9.4 us -> 0 us
  other arithmetic: 4.13 us -> 0 us
    pallas_call x0 -> x1, Pallas kernels: none -> 71.8 us  [local(): pl.pallas_call(functools.partial(kernel, row_count, col_count, spread, bl...]
    all_to_all x2 -> x0, blocking collectives: 59.8 us -> none  [the longest x1 29.9 us: local(): lax.all_to_all(result.transpose(2, 1, 3, 0, 4, 5).reshape(devices, items,...]
    dot_general x5 -> x0, matrix products: 45.1 us -> none  [the longest x1 26.2 us: local(): jnp.dot(depth.reshape(tile_rows * tile_cols, -1), project_weight, preferr...]
    reshape x5 -> x1, local copies, waits for them, and re-layouts: 16.9 us -> 2.84 us  [local(): tokens.reshape(tile_rows, blocks, stride_cols, channels)]
    sub x1 -> x0, matrix products: 10.4 us -> none  [attend_groups(): soft = jax.nn.softmax(scores, axis=-1).astype(jnp.bfloat16)]
    ppermute x4 -> x0, starting transfers between devices: 10 us -> none  [the longest x2 5.58 us: extended(): lax.ppermute(head, axis, [((i + 1) % count, i) for i in range(ends)])]
    ppermute x4 -> x0, waiting for transfers between devices: 9.4 us -> none  [the longest x2 9.39 us: extended(): lax.ppermute(tail, axis, [(i, (i + 1) % count) for i in range(ends)])]
    convert_element_type x3 -> x0, local copies, waits for them, and re-layouts: 4.99 us -> none  [the longest x1 2.88 us: attend_groups(): projected.astype(jnp.bfloat16).reshape(count, members, 3, HEADS, HEAD_DIM)]
  transfers between devices with their start and end apart: 4 -> 0, of which waited for: 1 -> 0; matrix products, arithmetic and copies ran while one was open for 1% -> 0% of each run, Pallas kernels for 0% -> 0%
where the time goes in v1:
time: 76.2 us; the launch traced here: 76 us
  Pallas kernels  71.8 us (94%)
  local copies, waits for them, and re-layouts  4.15 us (5%)
    pallas_call x1, Pallas kernels, local(): pl.pallas_call(functools.partial(kernel, row_count, col_count, spread, bl...  71.8 us
    reshape x1, local copies, waits for them, and re-layouts, local(): tokens.reshape(tile_rows, blocks, stride_cols, channels)  2.84 us

profile of v1, /device:TPU:13, one launch (start us, length us, event | category | flops | bytes accessed | tf_op | source)
XLA Modules:
  0.0 76.0 jit_solution(5576555380253683788)
XLA Ops:
  0.0 0.0 copy-start
  0.0 0.0 copy-start.2
  0.0 0.0 copy-start.1
  0.0 2.8 %copy.11 = bf16[4,8,32,512]{3,1,2,0:T(8,128)(2,1)} copy(bf16[4,8,32,512]{3,2,1,0:T(8,128)(2,1)} %bitcast.14) | data formatting | bytes 2097152 | tf_op jit(solution)/shard_map/reshape | solution.py:382
  2.8 0.0 copy-done
  2.9 0.0 copy-done.2
  2.9 0.0 copy-done.1
  2.9 71.8 %shard_map.73 = bf16[4,256,512]{2,1,0:T(8,128)(2,1)S(1)} custom-call(bf16[4,256,512]{2,1,0:T(8,128)(2,1)} %bitcast.13, f32[3,3,2048]{2,1,0:T(4,128)S(1)} %copy-done.1, f32[1,512]{1,0:T(1,128)S(1)} %bitcast.12, bf16[512,2048]{1,0:T(8,128)(2,1)} %ew_hbm.1, bf16[2048,512]{1,0:T(8,128)(2,1)} %pw_hbm.1, bf16[512,1536]{1,0:T(8,128)(2,1)} %aw_hbm.1, ...), custom_call_target="tpu_custom_call" | custom-call | tf_op jit(solution)/shard_map/pallas_call | solution.py:386
  74.7 1.3 %copy.9 = bf16[4,8,32,512]{3,2,1,0:T(8,128)(2,1)} copy(bf16[4,8,32,512]{3,1,2,0:T(8,128)(2,1)S(1)} %bitcast.11) | data formatting | bytes 2097152 | tf_op jit(solution)/shard_map/transpose | solution.py:431
Async XLA Ops:
  0.0 2.9 %copy-start = (bf16[512,512]{1,0:T(8,128)(2,1)S(1)}, bf16[512,512]{1,0:T(8,128)(2,1)}, u32[]{:S(2)}) copy-start(bf16[512,512]{1,0:T(8,128)(2,1)} %ow_hbm.1) | copy-start | bytes 1572868
  0.0 2.9 %copy-start.2 = (f32[512]{0:T(512)S(1)}, f32[512]{0:T(512)}, u32[]{:S(2)}) copy-start(f32[512]{0:T(512)} %param.11) | copy-start | bytes 6148
  0.0 2.9 %copy-start.1 = (f32[3,3,2048]{2,1,0:T(4,128)S(1)}, f32[3,3,2048]{2,1,0:T(4,128)}, u32[]{:S(2)}) copy-start(f32[3,3,2048]{2,1,0:T(4,128)} %dk_ref.1) | copy-start | bytes 221188

commit v2 on v1

--- a/solution.py
+++ b/solution.py
@@ -15,9 +15,8 @@
 MESH = pl.DeviceIdType.MESH
 
 
-def gelu_tanh(values):
-    half = 0.5 * values
-    inner = values * (0.7978845608028654 + 0.035677408136300125 * (values * values))
+def gelu_of_double(half):
+    inner = half * (1.5957691216057308 + 0.285419265090401 * (half * half))
     return half + half * jnp.tanh(inner)
 
 
@@ -42,6 +41,7 @@
     hrows,
     ledge,
     redge,
+    perm,
     xe,
     expanded,
     depth,
@@ -95,6 +95,20 @@
         return carry
 
     lax.fori_loop(1, total, greet, 0)
+
+    target = lax.broadcasted_iota(jnp.int32, perm.shape, 0)
+    origin = lax.broadcasted_iota(jnp.int32, perm.shape, 1)
+    residue = target // blocks
+    chosen = origin == (target - residue * blocks) * residues + residue
+    perm[...] = jnp.where(chosen, 0.5, 0.0).astype(jnp.bfloat16)
+
+    def permute(ext, source):
+        value = jnp.dot(perm[...], source[...], preferred_element_type=jnp.float32)
+        xe[ext, pl.ds(0, tile_tokens), :] = value.astype(jnp.bfloat16)
+
+    for ext in range(1, 4):
+        permute(ext, x_ref.at[ext - 1])
+
     pl.semaphore_wait(barrier, total - 1)
 
     last = tile_rows - 1
@@ -141,34 +155,28 @@
             def _():
                 halo_copy(i).wait_recv()
 
-    def stage(slot, source, ext):
+    def border(ext):
         place = lax.broadcasted_iota(jnp.int32, (blocks, channels), 0)
-        after = source[pl.ds(tile_tokens - edge, edge), :].astype(jnp.float32)[edge - blocks :]
-        before = source[pl.ds(0, edge), :].astype(jnp.float32)[:blocks]
-        low = ledge[ext].astype(jnp.float32)[edge - 1 : edge]
-        high = redge[ext].astype(jnp.float32)[0:1]
+        after = xe[ext, pl.ds(tile_tokens - edge, edge), :].astype(jnp.float32)[edge - blocks :]
+        before = xe[ext, pl.ds(0, edge), :].astype(jnp.float32)[:blocks]
+        low = 0.5 * ledge[ext].astype(jnp.float32)[edge - 1 : edge]
+        high = 0.5 * redge[ext].astype(jnp.float32)[0:1]
         low = jnp.where(place == 0, low, pltpu.roll(after, 1, 0))
         high = jnp.where(place == blocks - 1, high, pltpu.roll(before, blocks - 1, 0))
-        xe[slot, pl.ds(0, tile_tokens), :] = source[...]
-        xe[slot, pl.ds(tile_tokens, 2 * blocks), :] = jnp.concatenate([low, high], axis=0).astype(
+        xe[ext, pl.ds(tile_tokens, 2 * blocks), :] = jnp.concatenate([low, high], axis=0).astype(
             jnp.bfloat16
         )
 
     def expand(rows):
-        for slot, ext in enumerate(rows):
-            if ext == 0:
-                stage(slot, hrows.at[0], ext)
-            elif ext == tile_rows + 1:
-                stage(slot, hrows.at[1], ext)
-            else:
-                stage(slot, x_ref.at[ext - 1], ext)
+        for ext in rows:
+            border(ext)
         width = 256
 
         def columns(n, carry):
             lanes = pl.ds(pl.multiple_of(n * width, width), width)
-            for slot, ext in enumerate(rows):
-                product = jnp.dot(xe[slot], ew[:, lanes], preferred_element_type=jnp.float32)
-                product = gelu_tanh(product).reshape(residues + 2, blocks, width)
+            for ext in rows:
+                product = jnp.dot(xe[ext], ew[:, lanes], preferred_element_type=jnp.float32)
+                product = gelu_of_double(product).reshape(residues + 2, blocks, width)
                 expanded[ext, pl.ds(1, residues), :, lanes] = product[:residues]
                 expanded[ext, 0, :, lanes] = product[residues]
                 expanded[ext, residues + 1, :, lanes] = product[residues + 1]
@@ -181,7 +189,7 @@
 
         def channel(n, carry):
             lanes = pl.ds(pl.multiple_of(n * LANES, LANES), LANES)
-            taps = [[dk_ref[dr, pl.ds(dc, 1), lanes] for dc in range(3)] for dr in range(3)]
+            taps = [[0.5 * dk_ref[dr, pl.ds(dc, 1), lanes] for dc in range(3)] for dr in range(3)]
             for start in range(0, residues, part):
                 acc = None
                 for dr in range(3):
@@ -189,7 +197,7 @@
                     for dc in range(3):
                         term = window[dc : dc + part] * taps[dr][dc]
                         acc = term if acc is None else acc + term
-                value = gelu_tanh(acc).reshape(part * blocks, LANES).astype(jnp.bfloat16)
+                value = gelu_of_double(acc).reshape(part * blocks, LANES).astype(jnp.bfloat16)
                 depth[pl.ds(start * blocks, part * blocks), lanes] = value
             return carry
 
@@ -204,21 +212,18 @@
         lax.fori_loop(0, channels // width, project, 0)
         kind, step = i % kinds, i // kinds
         chunk = tile_tokens // 8
-
-        def norm(n, carry):
-            rows = pl.ds(pl.multiple_of(n * chunk, chunk), chunk)
-            value = (x_ref[i, rows, :].astype(jnp.float32) + branch[rows, :]).astype(jnp.bfloat16)
+        count = chunk // piece
+        for n in range(tile_tokens // chunk):
+            rows = pl.ds(n * chunk, chunk)
+            value = 2.0 * xe[i + 1, rows, :].astype(jnp.float32) + branch[rows, :]
+            value = value.astype(jnp.bfloat16)
             mb[i, rows, :] = value
             value = value.astype(jnp.float32)
             center = jnp.mean(value, axis=-1, keepdims=True)
             value = value - center
             scale = lax.rsqrt(jnp.mean(value * value, axis=-1, keepdims=True) + 1e-05)
             normed = (value * scale * gain_ref[...]).astype(jnp.bfloat16)
-            count = chunk // piece
             sendbuf[kind, step, pl.ds(n * count, count)] = normed.reshape(count, piece, channels)
-            return carry
-
-        lax.fori_loop(0, tile_tokens // chunk, norm, 0)
 
         def send(n, carry):
             other = lax.rem(own + n, team)
@@ -238,12 +243,12 @@
             device_id_type=MESH,
         )
 
-    def back_copy(kind, other, slot):
+    def back_copy(kind, group, other, slot):
         return pltpu.make_async_remote_copy(
-            src_ref=backbuf.at[kind, :, other],
-            dst_ref=retbuf.at[kind, :, slot],
-            send_sem=back_send.at[kind, other],
-            recv_sem=back_recv.at[kind, slot],
+            src_ref=backbuf.at[kind, group, other],
+            dst_ref=retbuf.at[kind, group, slot],
+            send_sem=back_send.at[kind, group, other],
+            recv_sem=back_recv.at[kind, group, slot],
             device_id=member(other),
             device_id_type=MESH,
         )
@@ -275,6 +280,7 @@
         per_block = LANES // HEAD_DIM
         head_of = lax.broadcasted_iota(jnp.int32, (members, LANES), 1) // HEAD_DIM
         ones = jnp.ones((members, LANES), jnp.bfloat16)
+        masks = [(head_of == h).astype(jnp.float32).astype(jnp.bfloat16) for h in range(per_block)]
         for g in range(group_count):
 
             def head_block(n, carry):
@@ -284,48 +290,49 @@
                 keys = qkv[g, :, pl.ds(pl.multiple_of(base + channels, LANES), LANES)]
                 values = qkv[g, :, pl.ds(pl.multiple_of(base + 2 * channels, LANES), LANES)]
                 values = jnp.concatenate([values, ones], axis=1)
-                result = jnp.zeros((members, LANES), jnp.float32)
-                for h in range(per_block):
-                    mask = (head_of == h).astype(jnp.float32).astype(jnp.bfloat16)
-                    scores = lax.dot_general(
-                        queries * mask,
-                        keys,
-                        (((1,), (1,)), ((), ())),
-                        preferred_element_type=jnp.float32,
-                    )
-                    top = jnp.max(scores, axis=-1, keepdims=True)
-                    soft = jnp.exp2(scores - top).astype(jnp.bfloat16)
-                    both = jnp.dot(soft, values, preferred_element_type=jnp.float32)
-                    result = jnp.where(head_of == h, both[:, :LANES] / both[:, LANES:], result)
-                heads[:, pl.ds(g * blocks, blocks), lanes] = result.reshape(
-                    per_kind * team, blocks, LANES
+                stacked = jnp.concatenate([queries * mask for mask in masks], axis=0)
+                scores = lax.dot_general(
+                    stacked, keys, (((1,), (1,)), ((), ())), preferred_element_type=jnp.float32
                 )
+                top = jnp.max(scores, axis=-1, keepdims=True)
+                soft = jnp.exp2(scores - top).astype(jnp.bfloat16)
+                both = jnp.dot(soft, values, preferred_element_type=jnp.float32)
+                both = both.reshape(per_block, members, 2 * LANES)
+                above, below = both[0, :, :LANES], both[0, :, LANES:]
+                for h in range(1, per_block):
+                    above = jnp.where(head_of == h, both[h, :, :LANES], above)
+                    below = jnp.where(head_of == h, both[h, :, LANES:], below)
+                heads[:, lanes] = (above / below).astype(jnp.bfloat16)
                 return carry
 
             lax.fori_loop(0, channels // LANES, head_block, 0)
-
-        merged = heads[...].reshape(per_kind * team * piece, channels).astype(jnp.bfloat16)
-        result = jnp.dot(merged, ow[...], preferred_element_type=jnp.float32)
-        backbuf[kind] = result.astype(jnp.bfloat16).reshape(per_kind, team, piece, channels)
-
-        def send(n, carry):
-            back_copy(kind, lax.rem(own + n, team), own).start()
-            return carry
-
-        lax.fori_loop(1, team, send, 0)
-        for step in range(per_kind):
-            retbuf[kind, step, own] = backbuf[kind, step, own]
+            result = jnp.dot(heads[...], ow[...], preferred_element_type=jnp.float32)
+            result = result.reshape(per_kind, team, blocks, channels)
+            result = jnp.concatenate([result[step] for step in range(per_kind)], axis=1)
+            backbuf[kind, g] = result.astype(jnp.bfloat16)
+
+            def send(n, carry):
+                back_copy(kind, g, lax.rem(own + n, team), own).start()
+                return carry
+
+            lax.fori_loop(1, team, send, 0)
+            retbuf[kind, g, own] = backbuf[kind, g, own]
 
     def finish(kind):
         def arrive(n, carry):
             other = lax.rem(own + n, team)
-            back_copy(kind, other, other).wait_recv()
+            for g in range(group_count):
+                back_copy(kind, g, other, other).wait_recv()
             return carry
 
         lax.fori_loop(1, team, arrive, 0)
         for step in range(per_kind):
             i = step * kinds + kind
-            attention = retbuf[kind, step].reshape(tile_tokens, channels).astype(jnp.float32)
+            attention = [
+                retbuf[kind, g].astype(jnp.float32)[:, step * blocks : (step + 1) * blocks]
+                for g in range(group_count)
+            ]
+            attention = jnp.concatenate(attention, axis=1).reshape(tile_tokens, channels)
             out_ref[i] = (mb[i].astype(jnp.float32) + attention).astype(jnp.bfloat16)
 
     weights[0].wait()
@@ -334,6 +341,10 @@
     weights[1].wait()
     mbconv_row(row_order[0])
     await_halo(range(2, len(halos)))
+    permute(0, hrows.at[0])
+    permute(tile_rows + 1, hrows.at[1])
+    for ext in range(4, tile_rows + 1):
+        permute(ext, x_ref.at[ext - 1])
     expand([*range(4, tile_rows + 2), 0])
     for i in row_order[1:]:
         mbconv_row(i)
@@ -356,7 +367,8 @@
         for kind in range(kinds):
             for step in range(per_kind):
                 forward_copy(kind, step, other, own).wait_send()
-            back_copy(kind, other, own).wait_send()
+            for g in range(group_count):
+                back_copy(kind, g, other, own).wait_send()
         return carry
 
     lax.fori_loop(1, team, drain, 0)
@@ -379,10 +391,9 @@
     piece = stride_cols // team * blocks
     row_order = [i for i in range(1, tile_rows) if i % kinds == 1 % kinds]
     row_order += [i for i in range(tile_rows - 1, -1, -1) if i not in row_order]
-    ordered = tokens.reshape(tile_rows, blocks, stride_cols, channels).transpose(0, 2, 1, 3)
-    ordered = ordered.reshape(tile_rows, tile_cols, channels)
     bf16, f32 = jnp.bfloat16, jnp.float32
     exchange = (kinds, per_kind, team, piece, channels)
+    returned = (kinds, piece // blocks, team, per_kind * blocks, channels)
     out = pl.pallas_call(
         functools.partial(kernel, row_count, col_count, spread, blocks, row_order),
         out_shape=jax.ShapeDtypeStruct((tile_rows, tile_cols, channels), bf16),
@@ -397,7 +408,8 @@
             pltpu.VMEM((2, tile_cols, channels), bf16),
             pltpu.VMEM((tile_rows + 2, 16, channels), bf16),
             pltpu.VMEM((tile_rows + 2, 16, channels), bf16),
-            pltpu.VMEM((3, tile_cols + 2 * blocks, channels), bf16),
+            pltpu.VMEM((tile_cols, tile_cols), bf16),
+            pltpu.VMEM((tile_rows + 2, tile_cols + 2 * blocks, channels), bf16),
             pltpu.VMEM((tile_rows + 2, stride_cols + 2, blocks, hidden), f32),
             pltpu.VMEM((tile_cols, hidden), bf16),
             pltpu.VMEM((tile_cols, channels), f32),
@@ -405,22 +417,22 @@
             pltpu.VMEM(exchange, bf16),
             pltpu.VMEM(exchange, bf16),
             pltpu.VMEM((piece // blocks, per_kind * team * blocks, 3 * channels), bf16),
-            pltpu.VMEM((per_kind * team, piece, channels), f32),
-            pltpu.VMEM(exchange, bf16),
-            pltpu.VMEM(exchange, bf16),
+            pltpu.VMEM((per_kind * team * blocks, channels), bf16),
+            pltpu.VMEM(returned, bf16),
+            pltpu.VMEM(returned, bf16),
             pltpu.SemaphoreType.DMA((4,)),
             pltpu.SemaphoreType.DMA((8,)),
             pltpu.SemaphoreType.DMA((8,)),
             pltpu.SemaphoreType.DMA((kinds, per_kind, team)),
             pltpu.SemaphoreType.DMA((kinds, per_kind, team)),
-            pltpu.SemaphoreType.DMA((kinds, team)),
-            pltpu.SemaphoreType.DMA((kinds, team)),
+            pltpu.SemaphoreType.DMA((kinds, piece // blocks, team)),
+            pltpu.SemaphoreType.DMA((kinds, piece // blocks, team)),
         ],
         compiler_params=pltpu.CompilerParams(
             collective_id=0, has_side_effects=True, vmem_limit_bytes=52 * 1024 * 1024
         ),
     )(
-        ordered,
+        tokens,
         depth_kernel,
         norm_gain.reshape(1, channels),
         expand_weight,

time: 76.2 us -> 75.6 us (level)
    reshape x1 -> x0, local copies, waits for them, and re-layouts: 2.84 us -> none  [local(): tokens.reshape(tile_rows, blocks, stride_cols, channels)]
    unnamed x6, local copies, waits for them, and re-layouts: 0.01 us -> 2.61 us
where the time goes in v2:
time: 75.6 us; the launch traced here: 75.3 us
  Pallas kernels  71.4 us (94%)
  local copies, waits for them, and re-layouts  3.91 us (5%)
    pallas_call x1, Pallas kernels, local(): pl.pallas_call(functools.partial(kernel, row_count, col_count, spread, bl...  71.4 us
    unnamed x6, local copies, waits for them, and re-layouts  2.61 us

profile of v2, /device:TPU:13, one launch (start us, length us, event | category | flops | bytes accessed | tf_op | source)
XLA Modules:
  0.0 75.3 jit_solution(27000626139179192)
XLA Ops:
  0.0 0.0 copy-start
  0.0 1.0 %copy-done = bf16[512,512]{1,0:T(8,128)(2,1)S(1)} copy-done((bf16[512,512]{1,0:T(8,128)(2,1)S(1)}, bf16[512,512]{1,0:T(8,128)(2,1)}, u32[]{:S(2)}) %copy-start) | copy-done | bytes 524312
  1.0 0.0 copy-start.1
  1.0 0.9 %copy-done.1 = f32[3,3,2048]{2,1,0:T(4,128)S(1)} copy-done((f32[3,3,2048]{2,1,0:T(4,128)S(1)}, f32[3,3,2048]{2,1,0:T(4,128)}, u32[]{:S(2)}) %copy-start.1) | copy-done | bytes 73752
  1.9 0.0 copy-start.2
  1.9 0.7 copy-done.2
  2.6 71.4 %shard_map.73 = bf16[4,256,512]{2,1,0:T(8,128)(2,1)S(1)} custom-call(bf16[4,256,512]{2,1,0:T(8,128)(2,1)} %x_ref.1, f32[3,3,2048]{2,1,0:T(4,128)S(1)} %copy-done.1, f32[1,512]{1,0:T(1,128)S(1)} %bitcast.6, bf16[512,2048]{1,0:T(8,128)(2,1)} %ew_hbm.1, bf16[2048,512]{1,0:T(8,128)(2,1)} %pw_hbm.1, bf16[512,1536]{1,0:T(8,128)(2,1)} %aw_hbm.1, ...), custom_call_target="tpu_custom_call" | custom-call | tf_op jit(solution)/shard_map/pallas_call | solution.py:397
  74.0 1.3 %copy.8 = bf16[4,8,32,512]{3,2,1,0:T(8,128)(2,1)} copy(bf16[4,8,32,512]{3,1,2,0:T(8,128)(2,1)S(1)} %bitcast.5) | data formatting | bytes 2097152 | tf_op jit(solution)/shard_map/transpose | solution.py:443
Async XLA Ops:
  0.0 1.0 %copy-start = (bf16[512,512]{1,0:T(8,128)(2,1)S(1)}, bf16[512,512]{1,0:T(8,128)(2,1)}, u32[]{:S(2)}) copy-start(bf16[512,512]{1,0:T(8,128)(2,1)} %ow_hbm.1) | copy-start | bytes 1572868
  1.0 0.9 %copy-start.1 = (f32[3,3,2048]{2,1,0:T(4,128)S(1)}, f32[3,3,2048]{2,1,0:T(4,128)}, u32[]{:S(2)}) copy-start(f32[3,3,2048]{2,1,0:T(4,128)} %dk_ref.1) | copy-start | bytes 221188
  1.9 0.7 copy-start.2

commit v3 on v2

--- a/solution.py
+++ b/solution.py
@@ -49,8 +49,10 @@
     mb,
     sendbuf,
     recvbuf,
-    qkv,
-    heads,
+    queries_t,
+    keys,
+    values_t,
+    heads_t,
     backbuf,
     retbuf,
     weight_sem,
@@ -266,47 +268,61 @@
         width = 256
 
         def projection(n, carry):
-            lanes = pl.ds(pl.multiple_of(n * width, width), width)
-            group_tokens = recvbuf[kind].reshape(per_kind * team * piece, channels)
-            value = jnp.dot(group_tokens, aw[:, lanes], preferred_element_type=jnp.float32)
-            value = value * jnp.where(n * width < channels, scale, 1.0)
-            value = value.reshape(per_kind * team, piece, width)
-            for g in range(group_count):
-                one = value[:, g * blocks : (g + 1) * blocks].reshape(members, width)
-                qkv[g, :, lanes] = one.astype(jnp.bfloat16)
-            return carry
-
-        lax.fori_loop(0, 3 * channels // width, projection, 0)
+            for part in range(3):
+                column = pl.multiple_of(part * channels + n * width, width)
+                place = pl.ds(pl.multiple_of(n * width, width), width)
+                group_tokens = recvbuf[kind].reshape(per_kind * team * piece, channels)
+                value = jnp.dot(
+                    group_tokens, aw[:, pl.ds(column, width)], preferred_element_type=jnp.float32
+                )
+                if part == 0:
+                    value = value * scale
+                value = value.reshape(per_kind * team, piece, width)
+                for g in range(group_count):
+                    one = value[:, g * blocks : (g + 1) * blocks].reshape(members, width)
+                    if part == 1:
+                        keys[g, :, place] = one.astype(jnp.bfloat16)
+                    else:
+                        store = queries_t if part == 0 else values_t
+                        store[g, place, :] = one.T.astype(jnp.bfloat16)
+            return carry
+
+        lax.fori_loop(0, channels // width, projection, 0)
         per_block = LANES // HEAD_DIM
-        head_of = lax.broadcasted_iota(jnp.int32, (members, LANES), 1) // HEAD_DIM
-        ones = jnp.ones((members, LANES), jnp.bfloat16)
-        masks = [(head_of == h).astype(jnp.float32).astype(jnp.bfloat16) for h in range(per_block)]
+        unrolled = 2
+        ones = jnp.ones((16, members), jnp.bfloat16)
+        zeros = jnp.zeros((HEAD_DIM, members), jnp.bfloat16)
         for g in range(group_count):
 
             def head_block(n, carry):
-                base = n * LANES
-                lanes = pl.ds(pl.multiple_of(base, LANES), LANES)
-                queries = qkv[g, :, lanes]
-                keys = qkv[g, :, pl.ds(pl.multiple_of(base + channels, LANES), LANES)]
-                values = qkv[g, :, pl.ds(pl.multiple_of(base + 2 * channels, LANES), LANES)]
-                values = jnp.concatenate([values, ones], axis=1)
-                stacked = jnp.concatenate([queries * mask for mask in masks], axis=0)
-                scores = lax.dot_general(
-                    stacked, keys, (((1,), (1,)), ((), ())), preferred_element_type=jnp.float32
-                )
-                top = jnp.max(scores, axis=-1, keepdims=True)
-                soft = jnp.exp2(scores - top).astype(jnp.bfloat16)
-                both = jnp.dot(soft, values, preferred_element_type=jnp.float32)
-                both = both.reshape(per_block, members, 2 * LANES)
-                above, below = both[0, :, :LANES], both[0, :, LANES:]
-                for h in range(1, per_block):
-                    above = jnp.where(head_of == h, both[h, :, :LANES], above)
-                    below = jnp.where(head_of == h, both[h, :, LANES:], below)
-                heads[:, lanes] = (above / below).astype(jnp.bfloat16)
+                for m in range(unrolled):
+                    base = pl.multiple_of((n * unrolled + m) * LANES, LANES)
+                    key_block = keys[g, :, pl.ds(base, LANES)]
+                    query_block = queries_t[g, pl.ds(base, LANES), :]
+                    value_block = values_t[g, pl.ds(base, LANES), :]
+                    for h in range(per_block):
+                        rows = slice(h * HEAD_DIM, (h + 1) * HEAD_DIM)
+                        query = [query_block[rows] if k == h else zeros for k in range(per_block)]
+                        scores = jnp.dot(
+                            key_block,
+                            jnp.concatenate(query, axis=0),
+                            preferred_element_type=jnp.float32,
+                        )
+                        top = jnp.max(scores, axis=0, keepdims=True)
+                        soft = jnp.exp2(scores - top).astype(jnp.bfloat16)
+                        both = jnp.dot(
+                            jnp.concatenate([value_block[rows], ones], axis=0),
+                            soft,
+                            preferred_element_type=jnp.float32,
+                        )
+                        heads_t[pl.ds(base + h * HEAD_DIM, HEAD_DIM), :] = both[:HEAD_DIM] * (
+                            1.0 / both[HEAD_DIM : HEAD_DIM + 1]
+                        )
                 return carry
 
-            lax.fori_loop(0, channels // LANES, head_block, 0)
-            result = jnp.dot(heads[...], ow[...], preferred_element_type=jnp.float32)
+            lax.fori_loop(0, channels // LANES // unrolled, head_block, 0)
+            merged = heads_t[...].T.astype(jnp.bfloat16)
+            result = jnp.dot(merged, ow[...], preferred_element_type=jnp.float32)
             result = result.reshape(per_kind, team, blocks, channels)
             result = jnp.concatenate([result[step] for step in range(per_kind)], axis=1)
             backbuf[kind, g] = result.astype(jnp.bfloat16)
@@ -416,8 +432,10 @@
             pltpu.VMEM((tile_rows, tile_cols, channels), bf16),
             pltpu.VMEM(exchange, bf16),
             pltpu.VMEM(exchange, bf16),
-            pltpu.VMEM((piece // blocks, per_kind * team * blocks, 3 * channels), bf16),
-            pltpu.VMEM((per_kind * team * blocks, channels), bf16),
+            pltpu.VMEM((piece // blocks, channels, per_kind * team * blocks), bf16),
+            pltpu.VMEM((piece // blocks, per_kind * team * blocks, channels), bf16),
+            pltpu.VMEM((piece // blocks, channels, per_kind * team * blocks), bf16),
+            pltpu.VMEM((channels, per_kind * team * blocks), f32),
             pltpu.VMEM(returned, bf16),
             pltpu.VMEM(returned, bf16),
             pltpu.SemaphoreType.DMA((4,)),
@@ -429,7 +447,7 @@
             pltpu.SemaphoreType.DMA((kinds, piece // blocks, team)),
         ],
         compiler_params=pltpu.CompilerParams(
-            collective_id=0, has_side_effects=True, vmem_limit_bytes=52 * 1024 * 1024
+            collective_id=0, has_side_effects=True, vmem_limit_bytes=62 * 1024 * 1024
         ),
     )(
         tokens,

time: 75.6 us -> 75.6 us (level)
  local copies, waits for them, and re-layouts: 3.91 us -> 2.52 us
  Pallas kernels: 71.4 us -> 72.6 us
    unnamed x6 -> x0, local copies, waits for them, and re-layouts: 2.61 us -> none
    transpose x1, local copies, waits for them, and re-layouts: 1.3 us -> 2.52 us  [local(): out.reshape(tile_rows, stride_cols, blocks, channels).transpose(0, 2, 1, 3)]
    pallas_call x1, Pallas kernels: 71.4 us -> 72.6 us  [local(): pl.pallas_call(functools.partial(kernel, row_count, col_count, spread, bl...]
where the time goes in v3:
time: 75.6 us; the launch traced here: 75.1 us
  Pallas kernels  72.6 us (96%)
  local copies, waits for them, and re-layouts  2.52 us (3%)
    pallas_call x1, Pallas kernels, local(): pl.pallas_call(functools.partial(kernel, row_count, col_count, spread, bl...  72.6 us
    transpose x1, local copies, waits for them, and re-layouts, local(): out.reshape(tile_rows, stride_cols, blocks, channels).transpose(0, 2, 1, 3)  2.52 us

profile of v3, /device:TPU:13, one launch (start us, length us, event | category | flops | bytes accessed | tf_op | source)
XLA Modules:
  0.0 75.1 jit_solution(10049516470556269979)
XLA Ops:
  0.0 72.6 %shard_map.73 = bf16[4,256,512]{2,1,0:T(8,128)(2,1)} custom-call(bf16[4,256,512]{2,1,0:T(8,128)(2,1)} %x_ref.1, f32[3,3,2048]{2,1,0:T(4,128)} %dk_ref.1, f32[1,512]{1,0:T(1,128)} %bitcast.6, bf16[512,2048]{1,0:T(8,128)(2,1)} %ew_hbm.1, bf16[2048,512]{1,0:T(8,128)(2,1)} %pw_hbm.1, bf16[512,1536]{1,0:T(8,128)(2,1)} %aw_hbm.1, bf16[512,512]{1,0:T(8,128)(2,1)} %ow_hbm.1), custom_call_target="tpu_custom_call" | custom-call | tf_op jit(solution)/shard_map/pallas_call | solution.py:413
  72.6 2.5 %copy.8 = bf16[4,8,32,512]{3,2,1,0:T(8,128)(2,1)} copy(bf16[4,8,32,512]{3,1,2,0:T(8,128)(2,1)} %bitcast.5) | data formatting | bytes 2097152 | tf_op jit(solution)/shard_map/transpose | solution.py:461
